TPU v7x, 256 devices: a whole 4x4x8 slice. The times are simulated.
256 devices in a mesh: grp: 8 (over z), leaf: 32 (over y, x, core).
Axes of the slice: x: 4, y: 4, z: 8, core: 2. Of those that a mesh axis runs over, the one named last changes fastest.
Arguments:
- configs: bfloat16 [524288, 64], P(('grp', 'leaf')), may hold values from -6 to 6, as said below
- order: int32 [256, 2048], P(('grp', 'leaf')), may hold values from 0 to 2047, each once within a row
- w_in: bfloat16 [64, 128], replicated, may hold values from -0.75 to 0.75
- bias_in: float32 [128], replicated, may hold values from -3 to 3
- w_out: bfloat16 [128, 128], replicated, may hold values from -0.5 to 0.5
- noise: float32 [524288], P(('grp', 'leaf')), may hold values from 0.2 to 2
- right_side: float32 [524288], P(('grp', 'leaf')), may hold values from -12 to 12, as said below
- near_blocks: int32 [2048, 6], P(('grp', 'leaf')), may hold values from 0 to 255
- near_live: int32 [2048, 6], P(('grp', 'leaf')), may hold values 0 or 1
- skeleton: int32 [8, 256], P('grp'), may hold values from 0 to 65535
Outputs:
- solution: float32 [524288], P(('grp', 'leaf'))
- residual: float32 [524288], P(('grp', 'leaf'))
Inputs may be any that keep to these rules, and one draw needn't show every extreme that they name: `configs`: configurations of order one. `right_side`: targets of order one.
All inputs are finite; a program needn't handle non-finite values. No bound on the sum of `near_live` on one device may be relied on, other than what follows from the above.
Results may differ from a plain program's by a relative error of at most 0.039.
Values may be sent and summed in bfloat16 or wider, within the bound.
A program may use at most 128 MiB of HBM per device.

v0:
```python
import jax
import jax.numpy as jnp
from jax import lax
from jax.sharding import PartitionSpec as P

BLK = 256
NEAR = 6
ITERS = 4
sharpness = 10.0
highest = lax.Precision.HIGHEST


def kernel_rows(left, right):
    inner = lax.dot_general(
        left, right, (((1,), (1,)), ((), ())), preferred_element_type=jnp.float32
    )
    return jnp.exp(sharpness * (inner - 1.0))


def features_of(inputs, w_in, bias_in, w_out):
    hidden = jnp.tanh(jnp.dot(inputs, w_in, preferred_element_type=jnp.float32) + bias_in).astype(
        jnp.bfloat16
    )
    raw = jnp.dot(hidden, w_out, preferred_element_type=jnp.float32)
    return (raw * lax.rsqrt(jnp.sum(raw * raw, -1, keepdims=True) + 1e-06)).astype(jnp.bfloat16)


def near_tiles(inputs):
    own_feat, part_feat, own_vec, part_vec, weights, out_weight = inputs
    self_tile = kernel_rows(own_feat, own_feat)
    cross = jnp.exp(
        sharpness
        * (jnp.einsum("if,kjf->kij", own_feat, part_feat, preferred_element_type=jnp.float32) - 1.0)
    )
    partner_tile = jnp.exp(
        sharpness
        * (
            jnp.einsum("kif,kjf->kij", part_feat, part_feat, preferred_element_type=jnp.float32)
            - 1.0
        )
    )
    own_out = out_weight * jnp.dot(self_tile, own_vec, precision=highest)
    own_out = own_out + jnp.sum(
        weights[:, None] * jnp.einsum("kij,kj->ki", cross, part_vec, precision=highest), 0
    )
    back = jnp.einsum("kij,i->kj", cross, own_vec, precision=highest) + jnp.einsum(
        "kij,kj->ki", partner_tile, part_vec, precision=highest
    )
    return (own_out, weights[:, None] * back)


def on_device(
    configs, order, w_in, bias_in, w_out, noise, right_side, near_blocks, near_live, skeleton
):
    row_count = configs.shape[0]
    blocks_dev = row_count // BLK
    tree_rows = jnp.take(configs, order[0], axis=0)
    own_features = features_of(tree_rows, w_in, bias_in, w_out)
    group_feat = lax.all_gather(own_features, "leaf", axis=0, tiled=True)
    group_blocks = group_feat.shape[0] // BLK
    skel_feat = jnp.take(group_feat, skeleton[0], axis=0)
    all_skel = lax.all_gather(skel_feat, "grp", axis=0, tiled=True)
    basis = kernel_rows(own_features, skel_feat)
    coupling = kernel_rows(skel_feat, all_skel)
    live_mask = near_live.astype(jnp.float32)
    out_weights = jnp.sum(live_mask, 1)
    flat_partners = near_blocks.reshape(-1)
    part_feat = jnp.take(group_feat.reshape(group_blocks, BLK, -1), flat_partners, axis=0).reshape(
        blocks_dev, NEAR, BLK, -1
    )
    own_blocks = own_features.reshape(blocks_dev, BLK, -1)
    picker = (jnp.arange(group_blocks, dtype=jnp.int32)[:, None] == flat_partners[None, :]).astype(
        jnp.float32
    )
    precond = 1.0 / (1.0 + noise)
    solution = jnp.zeros_like(right_side)
    residual = right_side

    def inner_total(left, right):
        return lax.psum(jnp.sum(left * right), ("grp", "leaf"))

    scaled = residual * precond
    direction = scaled
    product_now = inner_total(residual, scaled)
    for step in range(ITERS):
        whole = lax.all_gather(direction, "leaf", axis=0, tiled=True)
        part_vec = jnp.take(whole.reshape(group_blocks, BLK), near_blocks, axis=0)
        own_out, back = lax.map(
            near_tiles,
            (
                own_blocks,
                part_feat,
                direction.reshape(blocks_dev, BLK),
                part_vec,
                live_mask,
                out_weights,
            ),
        )
        back_flat = back.reshape(-1, BLK)
        returned = lax.psum_scatter(
            jnp.dot(picker, back_flat, precision=highest).astype(jnp.bfloat16),
            "leaf",
            scatter_dimension=0,
            tiled=True,
        ).astype(jnp.float32)
        apply_local_charge = jnp.dot(direction, basis, precision=highest)
        group_total = lax.psum(apply_local_charge, "leaf")
        charges = lax.all_gather(group_total[None, :], "grp", axis=0, tiled=True)
        field = jnp.dot(coupling, charges.reshape(-1), precision=highest)
        far_part = jnp.dot(basis, field, precision=highest)
        image = (own_out + returned).reshape(-1) + far_part + noise * direction
        step_size = product_now / inner_total(direction, image)
        solution = solution + step_size * direction
        residual = residual - step_size * image
        if step + 1 < ITERS:
            scaled = residual * precond
            product_next = inner_total(residual, scaled)
            direction = scaled + product_next / product_now * direction
            product_now = product_next
    return (solution, residual)


def solution(mesh):
    in_specs = (
        P(("grp", "leaf"), None),
        P(("grp", "leaf"), None),
        P(),
        P(),
        P(),
        P(("grp", "leaf")),
        P(("grp", "leaf")),
        P(("grp", "leaf"), None),
        P(("grp", "leaf"), None),
        P("grp", None),
    )
    out_specs = (P(("grp", "leaf")), P(("grp", "leaf")))
    return jax.shard_map(
        on_device, mesh=mesh, in_specs=in_specs, out_specs=out_specs, check_vma=False
    )
```

profile of v0, /device:TPU:1, one launch (start us, length us, event | category | flops | bytes accessed | tf_op | source)
XLA Modules:
  0.0 1393.6 jit_solution(11065837192118993395)
XLA Ops:
  9.9 6.2 gather_fusion
  18.3 26.4 %all_gather.31 = f32[65536]{0:T(1024)S(1)} all-gather(f32[2048]{0:T(1024)S(1)} %fusion.156), channel_id=1, replica_groups=mesh['grp'=8,'leaf'=32] {'leaf'}, dimensions={0}, use_global_device_ids=true | all-gather | bytes 270336 | tf_op jit(solution)/shard_map/all_gather | solution.py:86
  45.9 54.2 %all-gather.6.cloned.1.call-done = bf16[65536,128]{1,0:T(8,128)(2,1)} async-done(((bf16[2048,128]{1,0:T(8,128)(2,1)}), bf16[65536,128]{1,0:T(8,128)(2,1)}) %all-gather.6.cloned.1.call-update) | async-done | bytes 16777232 | tf_op jit(solution)/shard_map/all_gather | solution.py:59
  100.1 8.7 gather_fusion.2
  108.9 1.8 fusion.135
  110.7 20.9 %all_gather.32 = bf16[2048,128]{1,0:T(8,128)(2,1)S(1)} all-gather(bf16[256,128]{1,0:T(8,128)(2,1)S(1)} %broadcast_select_fusion.1), channel_id=1, replica_groups=mesh['grp'=8,'leaf'=32] {'grp'}, dimensions={0}, use_global_device_ids=true | all-gather | bytes 589824 | tf_op jit(solution)/shard_map/all_gather | solution.py:62
  131.6 8.5 gather_fusion.1
  140.1 3.9 broadcast_select_fusion
  144.0 71.0 %while.60 = (s32[]{:T(128)}, f32[8,256]{1,0:T(8,128)S(1)}, f32[8,6,256]{2,1,0:T(8,128)S(1)}, f32[8]{0:T(128)S(1)}, bf16[8,256,128]{2,1,0:T(8,128)(2,1)S(1)}, /*i...) while((s32[]{:T(128)}, f32[8,256]{1,0:T(8,128)S(1)}, ...), condition=%wide.region_6.8_spmd, body=%wide.region_4.7_spmd.sunk | while | flops 234756352 | bytes 9386733 | solution.py:88
  149.8 1.6 fusion.307
  158.6 1.6 fusion.307
  167.5 1.6 fusion.307
  176.4 1.6 fusion.307
  194.1 1.6 fusion.307
  203.0 1.6 fusion.307
  211.9 1.6 fusion.307
  216.0 1.8 fusion.133
  218.7 68.3 %psum.85 = f32[1,256]{1,0:T(1,128)S(1)} all-reduce(f32[1,256]{1,0:T(1,128)S(1)} %fusion.159), channel_id=1, replica_groups=mesh['grp'=8,'leaf'=32] {'leaf'}, use_global_device_ids=true, to_apply=%region_8.10 | all-reduce | flops 256 | bytes 2048 | tf_op jit(solution)/shard_map/psum | solution.py:107
  287.1 11.3 all-gather
  298.3 3.3 convolution_bitcast_fusion.3
  301.7 1.9 fusion.160
  304.8 74.9 %all-reduce = (f32[]{:T(128)}, f32[]{:T(128)}) all-reduce(f32[]{:T(128)} %get-tuple-element.568, f32[]{:T(128)} %get-tuple-element.567), channel_id=1, replica_groups=mesh['grp'=8,'leaf'=32] {'grp','leaf'}, use_global_device_ids=true, to_apply=%region_1.2 | all-reduce | flops 2 | bytes 16 | tf_op jit(solution)/shard_map/psum | solution.py:80
  381.7 74.4 %psum.87 = f32[]{:T(128)} all-reduce(f32[]{:T(128)} %get-tuple-element.647), channel_id=1, replica_groups=mesh['grp'=8,'leaf'=32] {'grp','leaf'}, use_global_device_ids=true, to_apply=%region_12.14 | all-reduce | flops 1 | bytes 8 | tf_op jit(solution)/shard_map/psum | solution.py:80
  457.5 25.0 %all_gather.34 = f32[65536]{0:T(1024)S(1)} all-gather(f32[2048]{0:T(1024)S(1)} %multiply_add_fusion.10), channel_id=1, replica_groups=mesh['grp'=8,'leaf'=32] {'leaf'}, dimensions={0}, use_global_device_ids=true | all-gather | bytes 270336 | tf_op jit(solution)/shard_map/all_gather | solution.py:86
  483.3 70.9 %while.61 = (s32[]{:T(128)}, f32[8,256]{1,0:T(8,128)S(1)}, f32[8,6,256]{2,1,0:T(8,128)S(1)}, f32[8]{0:T(128)S(1)}, bf16[8,256,128]{2,1,0:T(8,128)(2,1)S(1)}, /*i...) while((s32[]{:T(128)}, f32[8,256]{1,0:T(8,128)S(1)}, ...), condition=%wide.region_15.17_spmd, body=%wide.region_13.16_spmd.sunk | while | flops 234756352 | bytes 9386733 | solution.py:88
  497.9 1.6 fusion.327
  506.8 1.6 fusion.327
  515.7 1.6 fusion.327
  524.5 1.6 fusion.327
  533.4 1.6 fusion.327
  542.3 1.6 fusion.327
  551.1 1.6 fusion.327
  555.3 2.5 fusion.161
  557.8 62.3 %psum.88 = f32[1,256]{1,0:T(1,128)S(1)} all-reduce(f32[1,256]{1,0:T(1,128)S(1)} %fusion.161), channel_id=1, replica_groups=mesh['grp'=8,'leaf'=32] {'leaf'}, use_global_device_ids=true, to_apply=%region_17.19 | all-reduce | flops 256 | bytes 2048 | tf_op jit(solution)/shard_map/psum | solution.py:107
  620.1 10.8 all-gather.1
  630.9 3.3 convolution_bitcast_fusion.2
  634.2 1.9 fusion.162
  637.4 77.4 %psum.89 = f32[]{:T(128)} all-reduce(f32[]{:T(128)} %multiply_reduce_fusion.5), channel_id=1, replica_groups=mesh['grp'=8,'leaf'=32] {'grp','leaf'}, use_global_device_ids=true, to_apply=%region_19.21 | all-reduce | flops 1 | bytes 8 | tf_op jit(solution)/shard_map/psum | solution.py:80
  716.8 74.3 %psum.90 = f32[]{:T(128)} all-reduce(f32[]{:T(128)} %get-tuple-element.645), channel_id=1, replica_groups=mesh['grp'=8,'leaf'=32] {'grp','leaf'}, use_global_device_ids=true, to_apply=%region_21.23 | all-reduce | flops 1 | bytes 8 | tf_op jit(solution)/shard_map/psum | solution.py:80
  792.5 25.3 %all_gather.36 = f32[65536]{0:T(1024)S(1)} all-gather(f32[2048]{0:T(1024)S(1)} %multiply_add_fusion.8), channel_id=1, replica_groups=mesh['grp'=8,'leaf'=32] {'leaf'}, dimensions={0}, use_global_device_ids=true | all-gather | bytes 270336 | tf_op jit(solution)/shard_map/all_gather | solution.py:86
  818.6 71.0 %while.62 = (s32[]{:T(128)}, f32[8,256]{1,0:T(8,128)S(1)}, f32[8,6,256]{2,1,0:T(8,128)S(1)}, f32[8]{0:T(128)S(1)}, bf16[8,256,128]{2,1,0:T(8,128)(2,1)S(1)}, /*i...) while((s32[]{:T(128)}, f32[8,256]{1,0:T(8,128)S(1)}, ...), condition=%wide.region_24.26_spmd, body=%wide.region_22.25_spmd.sunk | while | flops 234756352 | bytes 9386733 | solution.py:88
  824.3 1.6 fusion.347
  842.1 1.6 fusion.347
  851.0 1.6 fusion.347
  859.8 1.6 fusion.347
  868.7 1.6 fusion.347
  877.6 1.6 fusion.347
  886.4 1.6 fusion.347
  890.6 2.5 fusion.163
  893.1 62.3 %psum.91 = f32[1,256]{1,0:T(1,128)S(1)} all-reduce(f32[1,256]{1,0:T(1,128)S(1)} %fusion.163), channel_id=1, replica_groups=mesh['grp'=8,'leaf'=32] {'leaf'}, use_global_device_ids=true, to_apply=%region_26.28 | all-reduce | flops 256 | bytes 2048 | tf_op jit(solution)/shard_map/psum | solution.py:107
  955.4 10.9 all-gather.2
  966.3 3.3 convolution_bitcast_fusion.1
  969.6 1.9 fusion.164
  972.8 77.3 %psum.92 = f32[]{:T(128)} all-reduce(f32[]{:T(128)} %multiply_reduce_fusion.3), channel_id=1, replica_groups=mesh['grp'=8,'leaf'=32] {'grp','leaf'}, use_global_device_ids=true, to_apply=%region_28.30 | all-reduce | flops 1 | bytes 8 | tf_op jit(solution)/shard_map/psum | solution.py:80
  1052.0 74.3 %psum.93 = f32[]{:T(128)} all-reduce(f32[]{:T(128)} %get-tuple-element.643), channel_id=1, replica_groups=mesh['grp'=8,'leaf'=32] {'grp','leaf'}, use_global_device_ids=true, to_apply=%region_30.32 | all-reduce | flops 1 | bytes 8 | tf_op jit(solution)/shard_map/psum | solution.py:80
  1127.7 25.1 %all_gather.38 = f32[65536]{0:T(1024)S(1)} all-gather(f32[2048]{0:T(1024)S(1)} %multiply_add_fusion.6), channel_id=1, replica_groups=mesh['grp'=8,'leaf'=32] {'leaf'}, dimensions={0}, use_global_device_ids=true | all-gather | bytes 270336 | tf_op jit(solution)/shard_map/all_gather | solution.py:86
  1153.6 70.9 %while.63 = (s32[]{:T(128)}, f32[8,256]{1,0:T(8,128)S(1)}, f32[8,6,256]{2,1,0:T(8,128)S(1)}, f32[8]{0:T(128)S(1)}, bf16[8,256,128]{2,1,0:T(8,128)(2,1)S(1)}, /*i...) while((s32[]{:T(128)}, f32[8,256]{1,0:T(8,128)S(1)}, ...), condition=%wide.region_33.35_spmd, body=%wide.region_31.34_spmd.sunk | while | flops 234756352 | bytes 9386733 | solution.py:88
  1159.3 1.6 fusion.367
  1225.5 2.5 fusion.165
  1228.0 62.4 %psum.94 = f32[1,256]{1,0:T(1,128)S(1)} all-reduce(f32[1,256]{1,0:T(1,128)S(1)} %fusion.165), channel_id=1, replica_groups=mesh['grp'=8,'leaf'=32] {'leaf'}, use_global_device_ids=true, to_apply=%region_35.37 | all-reduce | flops 256 | bytes 2048 | tf_op jit(solution)/shard_map/psum | solution.py:107
  1290.4 10.8 all-gather.3
  1301.2 3.3 convolution_bitcast_fusion
  1304.5 1.9 fusion.166
  1307.7 77.3 %psum.95 = f32[]{:T(128)} all-reduce(f32[]{:T(128)} %multiply_reduce_fusion.1), channel_id=1, replica_groups=mesh['grp'=8,'leaf'=32] {'grp','leaf'}, use_global_device_ids=true, to_apply=%region_37.39 | all-reduce | flops 1 | bytes 8 | tf_op jit(solution)/shard_map/psum | solution.py:80
  (544 shorter events, 267.7 us)
Async XLA Ops:
  7.2 8.9 copy-start
  7.2 92.9 %all-gather.6.cloned.1.call-start = ((), (), s32[]{:S(2)}) async-start(), calls=%async_computation.4 | async-start | bytes 17301504 | tf_op jit(solution)/shard_map/all_gather | solution.py:59
  9.9 6.2 copy-start.11
  9.9 6.2 copy-start.12
  16.8 1.3 copy-start.8
  16.8 1.4 copy-start.6
  16.8 1.4 copy-start.7
  16.8 1.5 copy-start.9
  16.9 28.7 %copy-start.10 = (s32[1,256]{1,0:T(1,128)S(1)}, s32[1,256]{1,0:T(1,128)}, u32[]{:S(2)}) copy-start(s32[1,256]{1,0:T(1,128)} %param.29) | copy-start | bytes 3076
  18.0 90.8 %copy-start.5 = (bf16[2048,128]{1,0:T(8,128)(2,1)S(1)}, bf16[2048,128]{1,0:T(8,128)(2,1)}, u32[]{:S(2)}) copy-start(bf16[2048,128]{1,0:T(8,128)(2,1)} %multiply_convert_fusion) | copy-start | bytes 1572868
  18.0 285.5 %reduce-scatter.5.cloned.1.call-start = ((), (), s32[]{:S(2)}) async-start(), calls=%async_computation.5 | async-start | bytes 135168 | tf_op jit(solution)/shard_map/reduce_scatter | solution.py:100
  215.0 2.8 copy-start.1
  215.9 420.2 %reduce-scatter.7.cloned.1.call-start = ((), (), s32[]{:S(2)}) async-start(), calls=%async_computation.6 | async-start | bytes 135168 | tf_op jit(solution)/shard_map/reduce_scatter | solution.py:100
  555.2 416.3 %reduce-scatter.9.cloned.1.call-start = ((), (), s32[]{:S(2)}) async-start(), calls=%async_computation.7 | async-start | bytes 135168 | tf_op jit(solution)/shard_map/reduce_scatter | solution.py:100
  557.8 76.5 %copy-start.2 = (f32[2048,256]{1,0:T(8,128)S(1)}, f32[2048,256]{1,0:T(8,128)}, u32[]{:S(2)}) copy-start(f32[2048,256]{1,0:T(8,128)} %fusion.135) | copy-start | bytes 6291460
  890.5 415.9 %reduce-scatter.11.cloned.1.call-start = ((), (), s32[]{:S(2)}) async-start(), calls=%async_computation.8 | async-start | bytes 135168 | tf_op jit(solution)/shard_map/reduce_scatter | solution.py:100
  893.1 76.5 %copy-start.3 = (f32[2048,256]{1,0:T(8,128)S(1)}, f32[2048,256]{1,0:T(8,128)}, u32[]{:S(2)}) copy-start(f32[2048,256]{1,0:T(8,128)} %fusion.135) | copy-start | bytes 6291460
  1228.0 76.5 %copy-start.4 = (f32[2048,256]{1,0:T(8,128)S(1)}, f32[2048,256]{1,0:T(8,128)}, u32[]{:S(2)}) copy-start(f32[2048,256]{1,0:T(8,128)} %fusion.135) | copy-start | bytes 6291460
Sparse Core Ops, SparseCore 0:
  18.2 81.8 all-gather.5
  216.1 82.5 reduce-scatter.4
  555.3 74.3 reduce-scatter.6
  890.6 74.4 reduce-scatter.8
  1225.6 74.4 reduce-scatter.10
where the time goes:
time: 1400 us; the launch traced here: 1390 us
  blocking collectives  952 us (68%)
  matrix products  271 us (19%)
  waiting for transfers between devices  54.3 us (4%)
  local copies, waits for them, and re-layouts  50.2 us (4%)
  other arithmetic  40.6 us (3%)
  between operations  23.8 us (2%)
    psum x7, blocking collectives, inner_total(): return lax.psum(jnp.sum(left * right), ('grp', 'leaf'))  530 us
    psum x4, blocking collectives, on_device(): group_total = lax.psum(apply_local_charge, 'leaf')  255 us
    all_gather x4, blocking collectives, on_device(): whole = lax.all_gather(direction, 'leaf', axis=0, tiled=True)  102 us
    all_gather x1, waiting for transfers between devices, on_device(): group_feat = lax.all_gather(own_features, 'leaf', axis=0, tiled=True)  54.2 us
    dot_general x32, matrix products, near_tiles(): jnp.einsum('kij,kj->ki', partner_tile, part_vec, precision=highest)  51.6 us
    dot_general x32, matrix products, near_tiles(): jnp.einsum('kif,kjf->kij', part_feat, part_feat, preferred_element_type=j...  47.5 us
    dot_general x32, matrix products, near_tiles(): jnp.einsum('kij,i->kj', cross, own_vec, precision=highest)  46.2 us
    dot_general x32, matrix products, near_tiles(): jnp.einsum('if,kjf->kij', own_feat, part_feat, preferred_element_type=jnp...  44.1 us
  transfers between devices with their start and end apart: 5, of which 1 were waited for; matrix products, arithmetic and copies ran while one was open for 2% of the time, Pallas kernels for 0%

commit v1 on v0

--- a/solution.py
+++ b/solution.py
@@ -56,7 +56,9 @@
     blocks_dev = row_count // BLK
     tree_rows = jnp.take(configs, order[0], axis=0)
     own_features = features_of(tree_rows, w_in, bias_in, w_out)
-    group_feat = lax.all_gather(own_features, "leaf", axis=0, tiled=True)
+    group_feat = jnp.concatenate(
+        lax.all_to_all(jnp.stack([own_features] * lax.axis_size("leaf")), "leaf", 0, 0), axis=0
+    )
     group_blocks = group_feat.shape[0] // BLK
     skel_feat = jnp.take(group_feat, skeleton[0], axis=0)
     all_skel = lax.all_gather(skel_feat, "grp", axis=0, tiled=True)

time: 1400 us -> 1790 us (1.28)
  blocking collectives: 952 us -> 1150 us
  waiting for transfers between devices: 54.3 us -> 231 us
    reduce_scatter x4, waiting for transfers between devices: 0.01 us -> 231 us  [on_device(): lax.psum_scatter(jnp.dot(picker, back_flat, precision=highest).astype(jnp...]
    all_gather x4, blocking collectives: 102 us -> 300 us  [on_device(): whole = lax.all_gather(direction, 'leaf', axis=0, tiled=True)]
    all_gather x1 -> x0, waiting for transfers between devices: 54.2 us -> none  [on_device(): group_feat = lax.all_gather(own_features, 'leaf', axis=0, tiled=True)]
  transfers between devices with their start and end apart: 5 -> 5, of which waited for: 1 -> 3; matrix products, arithmetic and copies ran while one was open for 2% -> 1% of each run, Pallas kernels for 0% -> 0%
where the time goes in v1:
time: 1790 us; the launch traced here: 1780 us
  blocking collectives  1150 us (64%)
  matrix products  262 us (15%)
  waiting for transfers between devices  231 us (13%)
  local copies, waits for them, and re-layouts  57.7 us (3%)
  other arithmetic  40 us (2%)
  between operations  23.8 us (1%)
    psum x7, blocking collectives, inner_total(): return lax.psum(jnp.sum(left * right), ('grp', 'leaf'))  528 us
    all_gather x4, blocking collectives, on_device(): whole = lax.all_gather(direction, 'leaf', axis=0, tiled=True)  300 us
    psum x4, blocking collectives, on_device(): group_total = lax.psum(apply_local_charge, 'leaf')  254 us
    reduce_scatter x4, waiting for transfers between devices, on_device(): lax.psum_scatter(jnp.dot(picker, back_flat, precision=highest).astype(jnp...  231 us
    dot_general x32, matrix products, near_tiles(): jnp.einsum('kij,kj->ki', partner_tile, part_vec, precision=highest)  51.6 us
    dot_general x32, matrix products, near_tiles(): jnp.einsum('kif,kjf->kij', part_feat, part_feat, preferred_element_type=j...  47.7 us
    dot_general x32, matrix products, near_tiles(): jnp.einsum('kij,i->kj', cross, own_vec, precision=highest)  45.8 us
    all_gather x4, blocking collectives, on_device(): charges = lax.all_gather(group_total[None, :], 'grp', axis=0, tiled=True)  45.4 us
  transfers between devices with their start and end apart: 5, of which 3 were waited for; matrix products, arithmetic and copies ran while one was open for 1% of the time, Pallas kernels for 0%

profile of v1, /device:TPU:1, one launch (start us, length us, event | category | flops | bytes accessed | tf_op | source)
XLA Modules:
  0.0 1777.2 jit_solution(17856306836448447433)
XLA Ops:
  9.9 6.2 gather_fusion
  17.1 6.2 stack.2
  23.3 8.8 all-to-all-start
  32.4 226.3 %all_gather.27 = f32[65536]{0:T(1024)S(1)} all-gather(f32[2048]{0:T(1024)S(1)} %fusion.156), channel_id=1, replica_groups=mesh['grp'=8,'leaf'=32] {'leaf'}, dimensions={0}, use_global_device_ids=true | all-gather | bytes 270336 | tf_op jit(solution)/shard_map/all_gather | solution.py:88
  259.8 8.7 gather_fusion.2
  269.0 23.6 %all_gather.28 = bf16[2048,128]{1,0:T(8,128)(2,1)S(1)} all-gather(bf16[256,128]{1,0:T(8,128)(2,1)S(1)} %broadcast_select_fusion.1), channel_id=1, replica_groups=mesh['grp'=8,'leaf'=32] {'grp'}, dimensions={0}, use_global_device_ids=true | all-gather | bytes 589824 | tf_op jit(solution)/shard_map/all_gather | solution.py:64
  292.7 8.5 gather_fusion.1
  301.1 3.9 broadcast_select_fusion
  305.0 71.1 %while.60 = (s32[]{:T(128)}, f32[8,256]{1,0:T(8,128)S(1)}, f32[8,6,256]{2,1,0:T(8,128)S(1)}, f32[8]{0:T(128)S(1)}, bf16[8,256,128]{2,1,0:T(8,128)(2,1)S(1)}, /*i...) while((s32[]{:T(128)}, f32[8,256]{1,0:T(8,128)S(1)}, ...), condition=%wide.region_6.8_spmd, body=%wide.region_4.7_spmd.sunk | while | flops 234756352 | bytes 9387233 | solution.py:90
  318.3 1.6 fusion.307
  327.2 1.6 fusion.307
  336.1 1.6 fusion.307
  345.0 1.6 fusion.307
  353.8 1.6 fusion.307
  371.6 1.6 fusion.307
  378.1 67.8 %psum.85 = f32[1,256]{1,0:T(1,128)S(1)} all-reduce(f32[1,256]{1,0:T(1,128)S(1)} %fusion.159), channel_id=1, replica_groups=mesh['grp'=8,'leaf'=32] {'leaf'}, use_global_device_ids=true, to_apply=%region_8.10 | all-reduce | flops 256 | bytes 2048 | tf_op jit(solution)/shard_map/psum | solution.py:109
  445.9 12.2 all-gather
  459.9 1.7 convolution_bitcast_fusion.3
  461.6 1.9 fusion.160
  464.8 74.7 %all-reduce = (f32[]{:T(128)}, f32[]{:T(128)}) all-reduce(f32[]{:T(128)} %get-tuple-element.568, f32[]{:T(128)} %get-tuple-element.567), channel_id=1, replica_groups=mesh['grp'=8,'leaf'=32] {'grp','leaf'}, use_global_device_ids=true, to_apply=%region_1.2 | all-reduce | flops 2 | bytes 16 | tf_op jit(solution)/shard_map/psum | solution.py:82
  541.5 74.5 %psum.87 = f32[]{:T(128)} all-reduce(f32[]{:T(128)} %get-tuple-element.647), channel_id=1, replica_groups=mesh['grp'=8,'leaf'=32] {'grp','leaf'}, use_global_device_ids=true, to_apply=%region_12.14 | all-reduce | flops 1 | bytes 8 | tf_op jit(solution)/shard_map/psum | solution.py:82
  617.3 25.0 %all_gather.30 = f32[65536]{0:T(1024)S(1)} all-gather(f32[2048]{0:T(1024)S(1)} %multiply_add_fusion.10), channel_id=1, replica_groups=mesh['grp'=8,'leaf'=32] {'leaf'}, dimensions={0}, use_global_device_ids=true | all-gather | bytes 270336 | tf_op jit(solution)/shard_map/all_gather | solution.py:88
  643.2 62.2 %psum.88 = f32[1,256]{1,0:T(1,128)S(1)} all-reduce(f32[1,256]{1,0:T(1,128)S(1)} %fusion.161), channel_id=1, replica_groups=mesh['grp'=8,'leaf'=32] {'leaf'}, use_global_device_ids=true, to_apply=%region_17.19 | all-reduce | flops 256 | bytes 2048 | tf_op jit(solution)/shard_map/psum | solution.py:109
  705.4 11.0 all-gather.1
  716.4 3.3 convolution_bitcast_fusion.2
  720.6 71.1 %while.61 = (s32[]{:T(128)}, f32[8,256]{1,0:T(8,128)S(1)}, f32[8,6,256]{2,1,0:T(8,128)S(1)}, f32[8]{0:T(128)S(1)}, bf16[8,256,128]{2,1,0:T(8,128)(2,1)S(1)}, /*i...) while((s32[]{:T(128)}, f32[8,256]{1,0:T(8,128)S(1)}, ...), condition=%wide.region_15.17_spmd, body=%wide.region_13.16_spmd.sunk | while | flops 234756352 | bytes 9387233 | solution.py:90
  733.8 1.6 fusion.327
  742.7 1.6 fusion.327
  751.6 1.6 fusion.327
  760.5 1.6 fusion.327
  769.4 1.6 fusion.327
  787.1 1.6 fusion.327
  792.7 1.9 fusion.162
  794.5 76.1 %reduce-scatter.7.cloned.1.call-done = bf16[8,256]{1,0:T(8,128)(2,1)} async-done(((bf16[256,256]{1,0:T(8,128)(2,1)}), bf16[8,256]{1,0:T(8,128)(2,1)}) %reduce-scatter.7.cloned.1.call-update) | async-done | bytes 4112 | tf_op jit(solution)/shard_map/reduce_scatter | solution.py:102
  872.0 77.5 %psum.89 = f32[]{:T(128)} all-reduce(f32[]{:T(128)} %multiply_reduce_fusion.5), channel_id=1, replica_groups=mesh['grp'=8,'leaf'=32] {'grp','leaf'}, use_global_device_ids=true, to_apply=%region_19.21 | all-reduce | flops 1 | bytes 8 | tf_op jit(solution)/shard_map/psum | solution.py:82
  951.4 73.3 %psum.90 = f32[]{:T(128)} all-reduce(f32[]{:T(128)} %get-tuple-element.645), channel_id=1, replica_groups=mesh['grp'=8,'leaf'=32] {'grp','leaf'}, use_global_device_ids=true, to_apply=%region_21.23 | all-reduce | flops 1 | bytes 8 | tf_op jit(solution)/shard_map/psum | solution.py:82
  1026.1 24.6 %all_gather.32 = f32[65536]{0:T(1024)S(1)} all-gather(f32[2048]{0:T(1024)S(1)} %multiply_add_fusion.8), channel_id=1, replica_groups=mesh['grp'=8,'leaf'=32] {'leaf'}, dimensions={0}, use_global_device_ids=true | all-gather | bytes 270336 | tf_op jit(solution)/shard_map/all_gather | solution.py:88
  1051.6 62.2 %psum.91 = f32[1,256]{1,0:T(1,128)S(1)} all-reduce(f32[1,256]{1,0:T(1,128)S(1)} %fusion.163), channel_id=1, replica_groups=mesh['grp'=8,'leaf'=32] {'leaf'}, use_global_device_ids=true, to_apply=%region_26.28 | all-reduce | flops 256 | bytes 2048 | tf_op jit(solution)/shard_map/psum | solution.py:109
  1113.8 11.1 all-gather.2
  1124.9 3.3 convolution_bitcast_fusion.1
  1129.0 71.1 %while.62 = (s32[]{:T(128)}, f32[8,256]{1,0:T(8,128)S(1)}, f32[8,6,256]{2,1,0:T(8,128)S(1)}, f32[8]{0:T(128)S(1)}, bf16[8,256,128]{2,1,0:T(8,128)(2,1)S(1)}, /*i...) while((s32[]{:T(128)}, f32[8,256]{1,0:T(8,128)S(1)}, ...), condition=%wide.region_24.26_spmd, body=%wide.region_22.25_spmd.sunk | while | flops 234756352 | bytes 9387233 | solution.py:90
  1133.4 1.6 fusion.347
  1142.3 1.6 fusion.347
  1151.2 1.6 fusion.347
  1160.1 1.6 fusion.347
  1169.0 1.6 fusion.347
  1177.8 1.6 fusion.347
  1186.7 1.6 fusion.347
  1195.6 1.6 fusion.347
  1201.2 1.9 fusion.164
  1203.0 77.3 %reduce-scatter.9.cloned.1.call-done = bf16[8,256]{1,0:T(8,128)(2,1)} async-done(((bf16[256,256]{1,0:T(8,128)(2,1)}), bf16[8,256]{1,0:T(8,128)(2,1)}) %reduce-scatter.9.cloned.1.call-update) | async-done | bytes 4112 | tf_op jit(solution)/shard_map/reduce_scatter | solution.py:102
  1281.6 77.5 %psum.92 = f32[]{:T(128)} all-reduce(f32[]{:T(128)} %multiply_reduce_fusion.3), channel_id=1, replica_groups=mesh['grp'=8,'leaf'=32] {'grp','leaf'}, use_global_device_ids=true, to_apply=%region_28.30 | all-reduce | flops 1 | bytes 8 | tf_op jit(solution)/shard_map/psum | solution.py:82
  1361.1 73.3 %psum.93 = f32[]{:T(128)} all-reduce(f32[]{:T(128)} %get-tuple-element.643), channel_id=1, replica_groups=mesh['grp'=8,'leaf'=32] {'grp','leaf'}, use_global_device_ids=true, to_apply=%region_30.32 | all-reduce | flops 1 | bytes 8 | tf_op jit(solution)/shard_map/psum | solution.py:82
  1435.7 24.3 %all_gather.34 = f32[65536]{0:T(1024)S(1)} all-gather(f32[2048]{0:T(1024)S(1)} %multiply_add_fusion.6), channel_id=1, replica_groups=mesh['grp'=8,'leaf'=32] {'leaf'}, dimensions={0}, use_global_device_ids=true | all-gather | bytes 270336 | tf_op jit(solution)/shard_map/all_gather | solution.py:88
  1461.0 62.2 %psum.94 = f32[1,256]{1,0:T(1,128)S(1)} all-reduce(f32[1,256]{1,0:T(1,128)S(1)} %fusion.165), channel_id=1, replica_groups=mesh['grp'=8,'leaf'=32] {'leaf'}, use_global_device_ids=true, to_apply=%region_35.37 | all-reduce | flops 256 | bytes 2048 | tf_op jit(solution)/shard_map/psum | solution.py:109
  1523.2 11.1 all-gather.3
  1534.3 3.3 convolution_bitcast_fusion
  1538.5 71.1 %while.63 = (s32[]{:T(128)}, f32[8,256]{1,0:T(8,128)S(1)}, f32[8,6,256]{2,1,0:T(8,128)S(1)}, f32[8]{0:T(128)S(1)}, bf16[8,256,128]{2,1,0:T(8,128)(2,1)S(1)}, /*i...) while((s32[]{:T(128)}, f32[8,256]{1,0:T(8,128)S(1)}, ...), condition=%wide.region_33.35_spmd, body=%wide.region_31.34_spmd.sunk | while | flops 234756352 | bytes 9387233 | solution.py:90
  1542.8 1.6 fusion.367
  1551.7 1.6 fusion.367
  1560.6 1.6 fusion.367
  1610.5 1.9 fusion.166
  1612.3 77.3 %reduce-scatter.11.cloned.1.call-done = bf16[8,256]{1,0:T(8,128)(2,1)} async-done(((bf16[256,256]{1,0:T(8,128)(2,1)}), bf16[8,256]{1,0:T(8,128)(2,1)}) %reduce-scatter.11.cloned.1.call-update) | async-done | bytes 4112 | tf_op jit(solution)/shard_map/reduce_scatter | solution.py:102
  1690.9 77.5 %psum.95 = f32[]{:T(128)} all-reduce(f32[]{:T(128)} %multiply_reduce_fusion.1), channel_id=1, replica_groups=mesh['grp'=8,'leaf'=32] {'grp','leaf'}, use_global_device_ids=true, to_apply=%region_37.39 | all-reduce | flops 1 | bytes 8 | tf_op jit(solution)/shard_map/psum | solution.py:82
  (536 shorter events, 270.4 us)
Async XLA Ops:
  7.2 8.9 copy-start
  9.8 6.2 copy-start.7
  9.8 6.2 copy-start.8
  23.3 8.9 copy-start.4
  23.3 9.0 copy-start.2
  23.3 9.0 copy-start.3
  23.3 236.5 %all-to-all-start = ((bf16[32,2048,128]{2,1,0:T(8,128)(2,1)}), bf16[32,2048,128]{2,1,0:T(8,128)(2,1)}, u32[]{:S(2)}, u32[]{:S(2)}) async-start(bf16[32,2048,128]{2,1,0:T(8,128)(2,1)} %stack.2), calls=%async_computation | async-start | bytes 33554432 | tf_op jit(solution)/shard_map/all_to_all | solution.py:60
  32.1 227.4 %copy-start.5 = (s32[8,6]{1,0:T(8,128)S(1)}, s32[8,6]{1,0:T(8,128)}, u32[]{:S(2)}) copy-start(s32[8,6]{1,0:T(8,128)} %param.28) | copy-start | bytes 580
  32.1 227.4 %copy-start.6 = (s32[1,256]{1,0:T(1,128)S(1)}, s32[1,256]{1,0:T(1,128)}, u32[]{:S(2)}) copy-start(s32[1,256]{1,0:T(1,128)} %param.29) | copy-start | bytes 3076
  32.2 431.3 %reduce-scatter.5.cloned.1.call-start = ((), (), s32[]{:S(2)}) async-start(), calls=%async_computation.5 | async-start | bytes 135168 | tf_op jit(solution)/shard_map/reduce_scatter | solution.py:102
  377.1 493.6 %reduce-scatter.7.cloned.1.call-start = ((), (), s32[]{:S(2)}) async-start(), calls=%async_computation.6 | async-start | bytes 135168 | tf_op jit(solution)/shard_map/reduce_scatter | solution.py:102
  458.5 1.4 copy-start.1
  792.6 487.7 %reduce-scatter.9.cloned.1.call-start = ((), (), s32[]{:S(2)}) async-start(), calls=%async_computation.7 | async-start | bytes 135168 | tf_op jit(solution)/shard_map/reduce_scatter | solution.py:102
  1201.1 488.5 %reduce-scatter.11.cloned.1.call-start = ((), (), s32[]{:S(2)}) async-start(), calls=%async_computation.8 | async-start | bytes 135168 | tf_op jit(solution)/shard_map/reduce_scatter | solution.py:102
Sparse Core Ops, SparseCore 0:
  377.2 82.1 reduce-scatter.4
  792.8 77.8 reduce-scatter.6
  1201.2 79.0 reduce-scatter.8
  1610.6 78.9 reduce-scatter.10
